TPU v7x, 1024 devices: a whole 4x8x16 slice. The times are simulated.
1024 devices in a mesh: ctx: 64 (over y_hi, z), exp: 8 (over x, core), rep: 2 (over y_lo).
Axes of the slice: x: 4, y: 8 (y_hi: 4, y_lo: 2; y = y_hi * 2 + y_lo), z: 16, core: 2. Of those that a mesh axis runs over, the one named last changes fastest.
Arguments:
- queries: bfloat16 [4096, 64, 576], P(('rep', 'exp'), 'ctx'), parts along dimension 0, may hold values from -2048 to 2048
- latents: bfloat16 [4096, 576], P(('rep', 'exp')), parts along dimension 0, may hold values from -6 to 6
- out_grad: bfloat16 [4096, 64, 512], P(('rep', 'exp'), 'ctx'), parts along dimension 0, may hold values from -24 to 24
Outputs:
- attended: bfloat16 [4096, 64, 512], P(('rep', 'exp'), 'ctx'), parts along dimension 0
- query_grad: float32 [4096, 64, 576], P(('rep', 'exp'), 'ctx'), parts along dimension 0
- latent_grad: float32 [4096, 576], P(('rep', 'exp')), parts along dimension 0
There are 2 independent parts, one for each index of `rep`. A program takes and returns all parts, laid end to end along the dimension named above; each array names one. Nothing has to cross between parts.
All inputs are finite; a program needn't handle non-finite values.
Results may differ from a plain program's by a relative error of at most 0.013.
Values may be sent and summed in bfloat16 or wider, within the bound.
A program may use at most 64 MiB of HBM per device.

v0:
```python
import jax
import jax.numpy as jnp
from jax import lax
from jax.sharding import PartitionSpec as P

score_scale = 192.0 ** (-0.5)


def body(queries, latents, out_grad):
    tok_rows, head_count, feature_width = queries.shape
    latent_width = out_grad.shape[2]
    rope_width = feature_width - latent_width
    flat_rows = tok_rows * head_count
    seq_groups = lax.axis_size("exp")
    sequence_rows = tok_rows * seq_groups
    flat_query = queries.reshape(flat_rows, feature_width)
    flat_grad = out_grad.reshape(flat_rows, latent_width)
    query_pos = (
        lax.axis_index("exp") * tok_rows + jnp.arange(flat_rows, dtype=jnp.int32) // head_count
    )
    allowed = jnp.arange(sequence_rows, dtype=jnp.int32)[None, :] <= query_pos[:, None]
    key_rows = lax.all_gather(latents, "exp", axis=0, tiled=True)
    scores = jnp.dot(flat_query, key_rows.T, preferred_element_type=jnp.float32) * score_scale
    scores = jnp.where(allowed, scores, -1e30)
    row_top = jnp.max(scores, axis=1, keepdims=True)
    row_mass = jnp.sum(jnp.exp(scores - row_top), axis=1, keepdims=True)
    probs = jnp.where(allowed, jnp.exp(scores - (row_top + jnp.log(row_mass))), 0.0)
    weights = probs.astype(jnp.bfloat16)
    values = key_rows[:, :latent_width]
    context = jnp.dot(weights, values, preferred_element_type=jnp.float32)
    attended = context.astype(jnp.bfloat16).reshape(tok_rows, head_count, latent_width)
    prob_grad = jnp.dot(flat_grad, values.T, preferred_element_type=jnp.float32)
    row_delta = jnp.sum(flat_grad.astype(jnp.float32) * context, axis=1, keepdims=True)
    score_grad = (probs * (prob_grad - row_delta)).astype(jnp.bfloat16)
    query_grad = jnp.dot(score_grad, key_rows, preferred_element_type=jnp.float32) * score_scale
    query_grad = query_grad.reshape(tok_rows, head_count, feature_width)
    key_part = (
        jnp.einsum("rk,rw->kw", score_grad, flat_query, preferred_element_type=jnp.float32)
        * score_scale
    )
    value_part = jnp.einsum("rk,rw->kw", weights, flat_grad, preferred_element_type=jnp.float32)
    partial_grad = lax.psum_scatter(
        key_part + jnp.pad(value_part, ((0, 0), (0, rope_width))),
        "exp",
        scatter_dimension=0,
        tiled=True,
    )
    latent_grad = lax.psum(partial_grad, "ctx")
    return (attended, query_grad, latent_grad)


def solution(mesh):
    return jax.shard_map(
        body,
        mesh=mesh,
        in_specs=(
            P(("rep", "exp"), "ctx", None),
            P(("rep", "exp"), None),
            P(("rep", "exp"), "ctx", None),
        ),
        out_specs=(
            P(("rep", "exp"), "ctx", None),
            P(("rep", "exp"), "ctx", None),
            P(("rep", "exp"), None),
        ),
        check_vma=False,
    )
```

profile of v0, /device:TPU:40, one launch (start us, length us, event | category | flops | bytes accessed | tf_op | source)
XLA Modules:
  0.0 704.9 jit_solution(14401818746726014606)
XLA Ops:
  7.2 0.0 copy-start
  7.2 0.0 all-gather.2.cloned.1.call-start
  7.2 0.7 all-gather.2.cloned.1.call-update
  7.9 0.0 reduce-scatter.2.cloned.1.call-start
  8.0 49.1 %all-gather.2.cloned.1.call-done = bf16[2048,576]{0,1:T(8,128)(2,1)} async-done(((bf16[256,576]{0,1:T(8,128)(2,1)}), bf16[2048,576]{0,1:T(8,128)(2,1)}) %all-gather.2.cloned.1.call-update) | async-done | bytes 2359312 | tf_op jit(solution)/shard_map/all_gather | solution.py:22
  57.1 0.0 copy-done
  57.1 2.8 fusion.15
  59.9 0.0 copy-start.3
  59.9 0.4 exponential_reduce_fusion
  60.3 0.5 copy-done.3
  60.9 1.0 fusion.10
  61.9 0.6 copy-done.1
  62.5 1.5 multiply_reduce_fusion
  64.0 1.0 fusion.2
  65.1 0.0 copy-start.2
  65.1 1.0 copy-done.2
  66.1 3.0 pad_add_fusion
  69.1 0.0 reduce-scatter.2.cloned.1.call-update
  69.1 0.0 all-reduce.3.cloned.1.call-start
  69.1 51.0 %reduce-scatter.2.cloned.1.call-done = f32[256,576]{0,1:T(8,128)} async-done(((f32[2048,576]{0,1:T(8,128)}), f32[256,576]{0,1:T(8,128)}) %reduce-scatter.2.cloned.1.call-update) | async-done | bytes 589840 | tf_op jit(solution)/shard_map/reduce_scatter | solution.py:42
  120.1 0.0 all-reduce.3.cloned.1.call-update
  120.1 2.9 fusion.7
  123.0 573.4 %all-reduce.3.cloned.1.call-done = f32[256,576]{0,1:T(8,128)} async-done(((f32[256,576]{0,1:T(8,128)}), f32[256,576]{0,1:T(8,128)}) %all-reduce.3.cloned.1.call-update) | async-done | bytes 589840 | tf_op jit(solution)/shard_map/psum | solution.py:48
  696.4 1.9 copy.7
  (3 shorter events, 0.0 us)
Async XLA Ops:
  7.2 49.9 %copy-start = (bf16[256,1,576]{0,2,1:T(8,128)(2,1)S(1)}, bf16[256,1,576]{0,2,1:T(8,128)(2,1)}, u32[]{:S(2)}) copy-start(bf16[256,1,576]{0,2,1:T(8,128)(2,1)} %param.3) | copy-start | bytes 884740
  7.2 49.9 %all-gather.2.cloned.1.call-start = ((), (), s32[]{:S(2)}) async-start(), calls=%async_computation.1 | async-start | bytes 2654208 | tf_op jit(solution)/shard_map/all_gather | solution.py:22
  7.9 112.2 %reduce-scatter.2.cloned.1.call-start = ((), (), s32[]{:S(2)}) async-start(), calls=%async_computation.2 | async-start | bytes 5308416 | tf_op jit(solution)/shard_map/reduce_scatter | solution.py:42
  59.9 1.0 copy-start.3
  60.9 1.7 copy-start.1
  65.1 1.0 copy-start.2
  69.1 627.3 %all-reduce.3.cloned.1.call-start = ((), (), s32[]{:S(2)}) async-start(), calls=%async_computation.3 | async-start | bytes 1179648 | tf_op jit(solution)/shard_map/psum | solution.py:48
Sparse Core Ops, SparseCore 0:
  10.7 46.3 all-gather.1
  69.2 50.8 reduce-scatter.1
  123.6 572.7 all-reduce.2
where the time goes:
time: 705 us
  waiting for transfers between devices  674 us (96%)
  between operations  13.8 us (2%)
  matrix products  12.2 us (2%)
    psum x1, waiting for transfers between devices, body(): latent_grad = lax.psum(partial_grad, 'ctx')  573 us
    reduce_scatter x1, waiting for transfers between devices, body(): lax.psum_scatter(key_part + jnp.pad(value_part, ((0, 0), (0, rope_width))...  51 us
    all_gather x1, waiting for transfers between devices, body(): key_rows = lax.all_gather(latents, 'exp', axis=0, tiled=True)  49.1 us
  transfers between devices with their start and end apart: 3, of which 3 were waited for; matrix products, arithmetic and copies ran while one was open for 0% of the time, Pallas kernels for 0%

commit v1 on v0

v1 whole, which is shorter than its diff:
```python
import functools

import jax
import jax.numpy as jnp
from jax import lax
from jax.experimental import pallas as pl
from jax.experimental.pallas import tpu as pltpu
from jax.sharding import PartitionSpec as P

MESH = pl.DeviceIdType.MESH
BF = jnp.bfloat16
F32 = jnp.float32
score_scale = 192.0 ** (-0.5)
NN = (((1,), (0,)), ((), ()))
NT = (((1,), (1,)), ((), ()))


def mm(a, b, dims=NN):
    return lax.dot_general(a, b, dims, preferred_element_type=F32)


def kernel(
    qt_ref, lt_ref, g_ref,
    att_ref, qg_ref, lg_ref,
    keys, qn, gt, sc, pg, ctx, row_m, row_l,
    sib_out, sib_in, hold, x_out, x_in, total,
    s1_out, s1_in, part1, s2_out, s2_in, part2, s3, g2, g1,
    ag_s, ag_r, fs_s, fs_r, cr_s, cr_r, xr_s, xr_r,
    s1_s, s1_r, s2_s, s2_r, s3_s, s3_r, g2_s, g2_r, g1_s, g1_r,
):
    c = lax.axis_index("ctx")
    e = lax.axis_index("exp")
    yh, z = c // 16, c % 16
    zi, zo = z % 4, z // 4
    x, k = e // 2, e % 2
    feat, rows = lt_ref.shape
    lat = g_ref.shape[1]

    sib = {"exp": x * 2 + (1 - k)}

    def at_x(v):
        return {"exp": v * 2 + k}

    def at_y(v):
        return {"ctx": v * 16 + z}

    def at_zi(v):
        return {"ctx": yh * 16 + zo * 4 + v}

    def at_zo(v):
        return {"ctx": yh * 16 + v * 4 + zi}

    a_me = jnp.where(k == 0, yh, zi)
    b_me = jnp.where(k == 0, zi, yh)

    def at_a(v):
        return {"ctx": jnp.where(k == 0, v * 16 + z, yh * 16 + zo * 4 + v)}

    def at_b(v):
        return {"ctx": jnp.where(k == 0, yh * 16 + zo * 4 + v, v * 16 + z)}

    def rdma(src, dst, ssem, rsem, dev):
        return pltpu.make_async_remote_copy(
            src_ref=src, dst_ref=dst, send_sem=ssem, recv_sem=rsem, device_id=dev, device_id_type=MESH
        )

    barrier = pltpu.get_barrier_semaphore()
    pl.semaphore_signal(barrier, inc=1, device_id=sib, device_id_type=MESH)
    for d in (1, 2, 3):
        pl.semaphore_signal(barrier, inc=1, device_id=at_x((x + d) % 4), device_id_type=MESH)
        pl.semaphore_signal(barrier, inc=1, device_id=at_y((yh + d) % 4), device_id_type=MESH)
        pl.semaphore_signal(barrier, inc=1, device_id=at_zi((zi + d) % 4), device_id_type=MESH)
        pl.semaphore_signal(barrier, inc=1, device_id=at_zo((zo + d) % 4), device_id_type=MESH)
    pl.semaphore_wait(barrier, 13)

    def ag(src_x, dst_x):
        return rdma(lt_ref, keys.at[src_x * 2 + k], ag_s.at[dst_x], ag_r.at[src_x], at_x(dst_x))

    for v in (1, 2, 3):
        @pl.when(v > x)
        def _():
            ag(x, v).start()

    own_fwd = rdma(lt_ref, keys.at[x * 2], fs_s.at[x], fs_r.at[x], sib)

    @pl.when(k == 0)
    def _():
        own_fwd.start()

    keys[e] = lt_ref[...]
    qn[...] = qt_ref[...].T
    gt[...] = g_ref[...].T

    below = lax.broadcasted_iota(jnp.int32, (rows, rows), 1) <= lax.broadcasted_iota(jnp.int32, (rows, rows), 0)
    s = jnp.where(below, mm(qn[...], lt_ref[...]) * score_scale, -1e30)
    sc[e] = s
    m = jnp.max(s, axis=1, keepdims=True)
    p = jnp.exp(s - m)
    row_m[...] = m
    row_l[...] = jnp.sum(p, axis=1, keepdims=True)
    ctx[...] = mm(p.astype(BF), lt_ref[:lat, :], NT)
    pg[e] = mm(g_ref[...], lt_ref[:lat, :])

    def forward(j):
        s = mm(qn[...], keys[j]) * score_scale
        sc[j] = s
        m_old = row_m[...]
        m = jnp.maximum(m_old, jnp.max(s, axis=1, keepdims=True))
        p = jnp.exp(s - m)
        fade = jnp.exp(m_old - m)
        row_m[...] = m
        row_l[...] = row_l[...] * fade + jnp.sum(p, axis=1, keepdims=True)
        ctx[...] = ctx[...] * fade + mm(p.astype(BF), keys[j, :lat, :], NT)
        pg[j] = mm(g_ref[...], keys[j, :lat, :])

    @pl.when(k == 1)
    def _():
        own_fwd.wait_recv()
        forward(x * 2)

    def pass_on(v, side):
        blk = keys.at[v * 2 + side]
        return rdma(blk, blk, fs_s.at[v], fs_r.at[v], sib)

    def fwd_step(v, carry):
        rdma(lt_ref, keys.at[v * 2 + k], ag_s.at[v], ag_r.at[v], at_x(v)).wait_recv()
        pass_on(v, k).start()
        forward(v * 2 + k)
        pass_on(v, 1 - k).wait_recv()
        forward(v * 2 + 1 - k)
        return carry

    lax.fori_loop(0, x, fwd_step, 0)

    inv = 1.0 / row_l[...]
    context = ctx[...] * inv
    att_ref[...] = context.astype(BF)
    lse = row_m[...] + jnp.log(row_l[...])
    delta = jnp.sum(g_ref[...].astype(F32) * context, axis=1, keepdims=True)
    row_m[...] = lse
    row_l[...] = delta
    qg_ref[...] = jnp.zeros_like(qg_ref)

    def backward(j, store):
        p = jnp.exp(sc[j] - row_m[...])
        ds = (p * (pg[j] - row_l[...])).astype(BF)
        qg_ref[...] += mm(keys[j], ds, NT)
        store(0, lat, mm(qt_ref[:lat, :], ds) * score_scale + mm(gt[...], p.astype(BF)))
        store(lat, feat, mm(qt_ref[lat:, :], ds) * score_scale)

    def to_sib(v):
        return rdma(sib_out.at[v], sib_in.at[v], cr_s.at[v], cr_r.at[v], sib)

    def to_x(v, src):
        return rdma(x_out.at[v], x_in.at[src], xr_s.at[v], xr_r.at[src], at_x(v))

    def bwd_pair(v):
        def put_sib(lo, hi, val):
            sib_out[v, lo:hi, :] = val.astype(BF)

        def put_hold(lo, hi, val):
            hold[v, lo:hi, :] = val

        backward(v * 2 + 1 - k, put_sib)
        to_sib(v).start()
        backward(v * 2 + k, put_hold)

    def send_x(v):
        to_sib(v).wait_recv()
        x_out[v] = (hold[v] + sib_in[v].astype(F32)).astype(BF)
        to_x(v, x).start()

    def bwd_step(v, carry):
        bwd_pair(v)

        @pl.when(v > 0)
        def _():
            send_x(v - 1)

        return carry

    lax.fori_loop(0, x, bwd_step, 0)

    @pl.when(k == 1)
    def _():
        def put_sib(lo, hi, val):
            sib_out[x, lo:hi, :] = val.astype(BF)

        backward(x * 2, put_sib)
        to_sib(x).start()

    @pl.when(x > 0)
    def _():
        send_x(x - 1)

    def put_total(lo, hi, val):
        total[lo:hi, :] = val

    backward(e, put_total)
    total[feat:, :] = jnp.zeros((total.shape[0] - feat, rows), F32)
    qg_ref[...] = qg_ref[...] * score_scale

    @pl.when(k == 0)
    def _():
        to_sib(x).wait_recv()
        total[:feat, :] += sib_in[x].astype(F32)

    def add_x(i, carry):
        v = 3 - i
        to_x(x, v).wait_recv()
        total[:feat, :] += x_in[v].astype(F32)
        return carry

    lax.fori_loop(0, 3 - x, add_x, 0)

    n1 = total.shape[0] // 4

    def c1(peer, src):
        return rdma(s1_out.at[peer], s1_in.at[src], s1_s.at[peer], s1_r.at[src], at_a(peer))

    for q in range(4):
        s1_out[q] = total[q * n1:(q + 1) * n1, :].astype(BF)
    for d in (1, 2, 3):
        c1((a_me + d) % 4, a_me).start()
    part1[...] = total[pl.ds(pl.multiple_of(a_me * n1, n1), n1), :]
    for d in (3, 2, 1):
        v = (a_me + d) % 4
        c1(a_me, v).wait_recv()
        part1[...] += s1_in[v].astype(F32)

    n2 = n1 // 2
    half = rows // 2

    def c2(peer, src):
        return rdma(s2_out.at[peer], s2_in.at[src], s2_s.at[peer], s2_r.at[src], at_b(peer))

    for q in range(4):
        lo, le = (q // 2) * n2, (q % 2) * half
        val = part1[lo:lo + n2, le:le + half]
        s2_out[q] = val.astype(BF)

        @pl.when(b_me == q)
        def _():
            part2[...] = val

    for d in (1, 2, 3):
        c2((b_me + d) % 4, b_me).start()
    for d in (3, 2, 1):
        v = (b_me + d) % 4
        c2(b_me, v).wait_recv()
        part2[...] += s2_in[v].astype(F32)

    def c3(peer, src):
        return rdma(s3.at[src], s3.at[src], s3_s.at[peer], s3_r.at[src], at_zo(peer))

    s3[zo] = part2[...].astype(BF)
    for d in (2, 1, 3):
        c3((zo + d) % 4, zo).start()
    for d in (1, 3, 2):
        c3(zo, (zo + d) % 4).wait_recv()
    g2[b_me] = (s3[0].astype(F32) + s3[1].astype(F32) + s3[2].astype(F32) + s3[3].astype(F32)).astype(BF)

    def c4(peer, src):
        return rdma(g2.at[src], g2.at[src], g2_s.at[peer], g2_r.at[src], at_b(peer))

    for d in (1, 2, 3):
        c4((b_me + d) % 4, b_me).start()
    for d in (3, 2, 1):
        c4(b_me, (b_me + d) % 4).wait_recv()
    for q in range(4):
        lo, le = (q // 2) * n2, (q % 2) * half
        g1[a_me, lo:lo + n2, le:le + half] = g2[q]

    def c5(peer, src):
        return rdma(g1.at[src], g1.at[src], g1_s.at[peer], g1_r.at[src], at_a(peer))

    for d in (1, 2, 3):
        c5((a_me + d) % 4, a_me).start()
    for d in (3, 2, 1):
        c5(a_me, (a_me + d) % 4).wait_recv()
    for q in range(4):
        hi = min(feat, (q + 1) * n1)
        lg_ref[q * n1:hi, :] = g1[q, :hi - q * n1, :].astype(F32)

    for v in (1, 2, 3):
        @pl.when(v > x)
        def _():
            ag(x, v).wait_send()

    @pl.when(k == 0)
    def _():
        own_fwd.wait_send()

    @pl.when(k == 1)
    def _():
        to_sib(x).wait_send()

    def drain(v, carry):
        pass_on(v, k).wait_send()
        to_sib(v).wait_send()
        to_x(v, x).wait_send()
        return carry

    lax.fori_loop(0, x, drain, 0)
    for d in (1, 2, 3):
        c1((a_me + d) % 4, a_me).wait_send()
        c2((b_me + d) % 4, b_me).wait_send()
        c3((zo + d) % 4, zo).wait_send()
        c4((b_me + d) % 4, b_me).wait_send()
        c5((a_me + d) % 4, a_me).wait_send()


def body(queries, latents, out_grad):
    rows, _, feat = queries.shape
    lat = out_grad.shape[2]
    padded = (feat + 127) // 128 * 128
    n1, n2 = padded // 4, padded // 8
    qt = queries.reshape(rows, feat).T
    vm = pltpu.VMEM
    sems = [pltpu.SemaphoreType.DMA((4,))] * 18
    att, qg, lg = pl.pallas_call(
        kernel,
        out_shape=(
            jax.ShapeDtypeStruct((rows, lat), BF),
            jax.ShapeDtypeStruct((feat, rows), F32),
            jax.ShapeDtypeStruct((feat, rows), F32),
        ),
        in_specs=[pl.BlockSpec(memory_space=pltpu.VMEM)] * 3,
        out_specs=[pl.BlockSpec(memory_space=pltpu.VMEM)] * 3,
        scratch_shapes=[
            vm((8, feat, rows), BF),
            vm((rows, feat), BF),
            vm((lat, rows), BF),
            vm((8, rows, rows), F32),
            vm((8, rows, rows), F32),
            vm((rows, lat), F32),
            vm((rows, 1), F32),
            vm((rows, 1), F32),
            vm((4, feat, rows), BF),
            vm((4, feat, rows), BF),
            vm((4, feat, rows), F32),
            vm((4, feat, rows), BF),
            vm((4, feat, rows), BF),
            vm((padded, rows), F32),
            vm((4, n1, rows), BF),
            vm((4, n1, rows), BF),
            vm((n1, rows), F32),
            vm((4, n2, rows // 2), BF),
            vm((4, n2, rows // 2), BF),
            vm((n2, rows // 2), F32),
            vm((4, n2, rows // 2), BF),
            vm((4, n2, rows // 2), BF),
            vm((4, n1, rows), BF),
        ] + sems,
        compiler_params=pltpu.CompilerParams(
            collective_id=0, has_side_effects=True, vmem_limit_bytes=48 * 2**20
        ),
    )(qt, latents.T, out_grad.reshape(rows, lat))
    return att.reshape(rows, 1, lat), qg.T.reshape(rows, 1, feat), lg.T


def solution(mesh):
    return jax.shard_map(
        body,
        mesh=mesh,
        in_specs=(
            P(("rep", "exp"), "ctx", None),
            P(("rep", "exp"), None),
            P(("rep", "exp"), "ctx", None),
        ),
        out_specs=(
            P(("rep", "exp"), "ctx", None),
            P(("rep", "exp"), "ctx", None),
            P(("rep", "exp"), None),
        ),
        check_vma=False,
    )
```

time: 705 us -> 95.6 us (0.14)
  the two profiles are of different devices: /device:TPU:40 before, /device:TPU:52 now
where the time goes in v1:
time: 95.6 us; the launch traced here: 95.4 us
  Pallas kernels  89.5 us (94%)
  local copies, waits for them, and re-layouts  5.2 us (5%)
    pallas_call x1, Pallas kernels, body(): pl.pallas_call(kernel, out_shape=(jax.ShapeDtypeStruct((rows, lat), BF),...  89.5 us
    unnamed x9, local copies, waits for them, and re-layouts  5.2 us

profile of v1, /device:TPU:52, one launch (start us, length us, event | category | flops | bytes accessed | tf_op | source)
XLA Modules:
  0.0 95.4 jit_solution(13768570187922133674)
XLA Ops:
  0.6 0.0 copy-start
  0.6 1.0 copy-done
  1.6 0.0 copy-start.1
  1.6 1.0 %copy-done.1 = bf16[256,576]{0,1:T(8,128)(2,1)S(1)} copy-done((bf16[256,576]{0,1:T(8,128)(2,1)S(1)}, bf16[256,576]{0,1:T(8,128)(2,1)}, u32[]{:S(2)}) %copy-start.1) | copy-done | bytes 294936
  2.6 0.0 copy-start.2
  2.6 0.9 copy-done.2
  3.5 89.5 %shard_map.58 = (bf16[256,512]{1,0:T(8,128)(2,1)S(1)}, f32[576,256]{1,0:T(8,128)S(1)}, f32[576,256]{1,0:T(8,128)S(1)}) custom-call(bf16[576,256]{1,0:T(8,128)(2,1)S(1)} %bitcast.12, bf16[576,256]{1,0:T(8,128)(2,1)S(1)} %bitcast.13, bf16[256,512]{1,0:T(8,128)(2,1)S(1)} %bitcast.14), custom_call_target="tpu_custom_call" | custom-call | tf_op jit(solution)/shard_map/pallas_call | solution.py:321
  93.0 0.7 copy.9
  93.7 0.8 copy.10
  94.5 0.8 copy.11
Async XLA Ops:
  0.6 1.0 %copy-start = (bf16[256,1,576]{0,2,1:T(8,128)(2,1)S(1)}, bf16[256,1,576]{0,2,1:T(8,128)(2,1)}, u32[]{:S(2)}) copy-start(bf16[256,1,576]{0,2,1:T(8,128)(2,1)} %param.3) | copy-start | bytes 884740
  1.6 1.0 %copy-start.1 = (bf16[256,576]{0,1:T(8,128)(2,1)S(1)}, bf16[256,576]{0,1:T(8,128)(2,1)}, u32[]{:S(2)}) copy-start(bf16[256,576]{0,1:T(8,128)(2,1)} %param.4) | copy-start | bytes 884740
  2.6 0.9 copy-start.2

commit v2 on v1

v2 whole, which is shorter than its diff:
```python
import functools

import jax
import jax.numpy as jnp
from jax import lax
from jax.experimental import pallas as pl
from jax.experimental.pallas import tpu as pltpu
from jax.sharding import PartitionSpec as P

MESH = pl.DeviceIdType.MESH
BF = jnp.bfloat16
F32 = jnp.float32
score_scale = 192.0 ** (-0.5)
NN = (((1,), (0,)), ((), ()))
NT = (((1,), (1,)), ((), ()))
(AG, AH, ZU, ZD, FS, CR, RU, RD, XR, S1, S3, G1, G0) = range(0, 26, 2)


def mm(a, b, dims=NN):
    return lax.dot_general(a, b, dims, preferred_element_type=F32)


def at(start, size):
    return pl.ds(pl.multiple_of(start, 16), size)


def kernel(
    qt_any, lt_any, g_any,
    att_any, qg_any, lg_any,
    att_ref, qg_ref, fin,
    qt_ref, lt_ref, g_ref,
    keys, qn, gt, sc, pg, ctx, row_m, row_l,
    sib_out, sib_in, hold, z_out, z_in, x_out, x_in, total,
    s1_out, s1_in, part, s3, g1,
    in_sem, out_sem, sem, far,
):
    c = lax.axis_index("ctx")
    e = lax.axis_index("exp")
    yh, z = c // 16, c % 16
    zi, zo = z % 4, z // 4
    h, r = z % 2, zi // 2
    x, k = e // 2, e % 2
    feat, rows = lt_ref.shape
    lat = g_ref.shape[1]
    n_half, n_quarter = feat // 2, feat // 4
    mine, other = h * n_half, (1 - h) * n_half

    loads = [
        pltpu.make_async_copy(src, dst, in_sem.at[i])
        for i, (src, dst) in enumerate(((lt_any, lt_ref), (qt_any, qt_ref), (g_any, g_ref)))
    ]
    for load in loads:
        load.start()
    stores = [
        pltpu.make_async_copy(src, dst, out_sem.at[i])
        for i, (src, dst) in enumerate(((att_ref, att_any), (qg_ref, qg_any), (fin, lg_any)))
    ]

    sib = {"exp": x * 2 + (1 - k)}
    up, down = {"ctx": yh * 16 + (z + 1) % 16}, {"ctx": yh * 16 + (z + 15) % 16}
    def at_x(v):
        return {"exp": v * 2 + k}

    def at_shard(v):
        return {"ctx": (v // 2) * 16 + zo * 4 + (v % 2) * 2 + h}

    own = yh * 2 + r

    def at_zo(v):
        return {"ctx": yh * 16 + v * 4 + zi}

    def rdma(src, dst, kind, i, j, dev):
        return pltpu.make_async_remote_copy(
            src_ref=src, dst_ref=dst, send_sem=sem.at[kind, i], recv_sem=sem.at[kind + 1, j],
            device_id=dev, device_id_type=MESH,
        )

    barrier = pltpu.get_barrier_semaphore()
    near = [sib, up, down, at_zo((zo + 1) % 4), at_zo((zo + 3) % 4)]
    near += [at_x((x + d) % 4) for d in (1, 2, 3)] + [at_shard((own + d) % 8) for d in range(1, 8)]
    for dev in near:
        pl.semaphore_signal(barrier, inc=1, device_id=dev, device_id_type=MESH)
    loads[0].wait()
    keys[e] = lt_ref[...]
    pl.semaphore_wait(barrier, len(near))
    pl.semaphore_signal(far, inc=1, device_id=at_zo((zo + 1) % 4), device_id_type=MESH)

    def ag(src_x, dst_x, piece):
        part = at(mine + piece * n_quarter, n_quarter)
        return rdma(
            lt_ref.at[part], keys.at[src_x * 2 + k, part], AG if piece == 0 else AH, dst_x, src_x, at_x(dst_x)
        )

    def pass_on(v, side):
        blk = keys.at[v * 2 + side]
        return rdma(blk, blk, FS, v, v, sib)

    def lift(v, base):
        blk = keys.at[v * 2 + k, at(base, n_quarter)]
        return rdma(blk, blk, ZU, v, v, up)

    def lower(v, base):
        blk = keys.at[v * 2 + k, at(base + n_quarter, n_quarter)]
        return rdma(blk, blk, ZD, v, v, down)

    own_fwd = rdma(lt_ref, keys.at[x * 2], FS, x, x, sib)

    for piece in (0, 1):
        @pl.when(x < 3)
        def _():
            ag(x, x + 1, piece).start()

        @pl.when(x == 0)
        def _():
            ag(x, x + 3, piece).start()

    @pl.when(k == 0)
    def _():
        own_fwd.start()

    loads[1].wait()
    qn[...] = qt_ref[...].T
    loads[2].wait()
    gt[...] = g_ref[...].T

    below = lax.broadcasted_iota(jnp.int32, (rows, rows), 1) <= lax.broadcasted_iota(jnp.int32, (rows, rows), 0)
    s = jnp.where(below, mm(qn[...], lt_ref[...]) * score_scale, -1e30)
    sc[e] = s
    m = jnp.max(s, axis=1, keepdims=True)
    p = jnp.exp(s - m)
    row_m[...] = m
    row_l[...] = jnp.sum(p, axis=1, keepdims=True)
    ctx[...] = mm(p.astype(BF), lt_ref[:lat, :], NT)
    pg[e] = mm(g_ref[...], lt_ref[:lat, :])

    @pl.when(x < 2)
    def _():
        for piece in (0, 1):
            ag(x, x + 1, piece).wait_send()

            @pl.when(x == 0)
            def _():
                ag(x, x + 3, piece).wait_send()

            ag(x, x + 2, piece).start()

    def forward(j):
        s = mm(qn[...], keys[j]) * score_scale
        sc[j] = s
        m_old = row_m[...]
        m = jnp.maximum(m_old, jnp.max(s, axis=1, keepdims=True))
        p = jnp.exp(s - m)
        fade = jnp.exp(m_old - m)
        row_m[...] = m
        row_l[...] = row_l[...] * fade + jnp.sum(p, axis=1, keepdims=True)
        ctx[...] = ctx[...] * fade + mm(p.astype(BF), keys[j, :lat, :], NT)
        pg[j] = mm(g_ref[...], keys[j, :lat, :])

    @pl.when(k == 1)
    def _():
        own_fwd.wait_recv()
        forward(x * 2)

    def gather_step(i, carry):
        v = x - jnp.where(i == 0, 1, jnp.where(i == 1, 3, 2))

        @pl.when((i < 3) & (v >= 0))
        def _():
            ag(v, x, 0).wait_recv()
            lift(v, mine).start()
            ag(v, x, 1).wait_recv()
            lower(v, mine).start()

        w = x - jnp.where(i == 1, 1, jnp.where(i == 2, 3, 2))

        @pl.when((i > 0) & (w >= 0))
        def _():
            lift(w, other).wait_recv()
            lower(w, other).wait_recv()
            pass_on(w, k).start()
            forward(w * 2 + k)
            pass_on(w, 1 - k).wait_recv()
            forward(w * 2 + 1 - k)

        return carry

    lax.fori_loop(0, 4, gather_step, 0)

    inv = 1.0 / row_l[...]
    context = ctx[...] * inv
    att_ref[...] = context.astype(BF)
    stores[0].start()
    lse = row_m[...] + jnp.log(row_l[...])
    delta = jnp.sum(g_ref[...].astype(F32) * context, axis=1, keepdims=True)
    row_m[...] = lse
    row_l[...] = delta
    qg_ref[...] = jnp.zeros_like(qg_ref)

    def backward(j, store):
        p = jnp.exp(sc[j] - row_m[...])
        ds = (p * (pg[j] - row_l[...])).astype(BF)
        qg_ref[...] += mm(keys[j], ds, NT)
        store(0, lat, mm(qt_ref[:lat, :], ds) * score_scale + mm(gt[...], p.astype(BF)))
        store(lat, feat, mm(qt_ref[lat:, :], ds) * score_scale)

    def to_sib(v):
        return rdma(sib_out.at[v], sib_in.at[v], CR, v, v, sib)

    def to_up(v):
        return rdma(z_out.at[v, pl.ds(n_quarter, n_quarter)], z_in.at[v, pl.ds(n_quarter, n_quarter)], RU, v, v, up)

    def to_down(v):
        return rdma(z_out.at[v, pl.ds(0, n_quarter)], z_in.at[v, pl.ds(0, n_quarter)], RD, v, v, down)

    def to_x(v, src):
        return rdma(x_out.at[v], x_in.at[src], XR, v, src, at_x(v))

    def order(i):
        return x - jnp.where(i == 0, 2, jnp.where(i == 1, 3, jnp.where(i == 2, 1, 0)))

    def bwd_step(i, carry):
        v = order(i)

        @pl.when((i < 4) & (v >= 0))
        def _():
            def put_sib(lo, hi, val):
                sib_out[v, lo:hi, :] = val.astype(BF)

            def put_hold(lo, hi, val):
                hold[v, lo:hi, :] = val

            @pl.when(v * 2 + 1 - k <= e)
            def _():
                backward(v * 2 + 1 - k, put_sib)
                to_sib(v).start()

            backward(v * 2 + k, put_hold)

        u = order(i - 1)

        @pl.when((i > 0) & (i < 5) & (u >= 0))
        def _():
            @pl.when(u * 2 + k <= x * 2 + 1 - k)
            def _():
                to_sib(u).wait_recv()
                hold[u] += sib_in[u].astype(F32)

            z_out[u] = hold[u, at(other, n_half), :].astype(BF)
            to_up(u).start()
            to_down(u).start()

        t = order(i - 2)

        @pl.when((i > 1) & (t >= 0))
        def _():
            to_down(t).wait_recv()
            to_up(t).wait_recv()
            val = hold[t, at(mine, n_half), :] + z_in[t].astype(F32)

            @pl.when(t < x)
            def _():
                x_out[t] = val.astype(BF)
                to_x(t, x).start()

            @pl.when(t == x)
            def _():
                total[...] = val

        return carry

    lax.fori_loop(0, 6, bwd_step, 0)
    qg_ref[...] = qg_ref[...] * score_scale
    stores[1].start()

    def add_x(i, carry):
        v = 3 - i
        to_x(x, v).wait_recv()
        total[...] += x_in[v].astype(F32)
        return carry

    lax.fori_loop(0, 3 - x, add_x, 0)

    half = rows // 2
    n1, n2 = n_half // 2, s1_out.shape[1]

    def c1(peer, src):
        return rdma(s1_out.at[peer], s1_in.at[src], S1, peer, src, at_shard(peer))

    for q in range(8):
        lo = (q // 4) * n1 + (q % 2) * (n1 - n2)
        val = total[lo:lo + n2, (q // 2 % 2) * half:(q // 2 % 2 + 1) * half]
        s1_out[q] = val.astype(BF)

        @pl.when(own == q)
        def _():
            part[...] = val

    hops = (4, 5, 3, 2, 6, 7, 1)
    for d in hops:
        c1((own + d) % 8, own).start()
    for d in hops[::-1]:
        v = (own + d) % 8
        c1(own, v).wait_recv()
        part[...] += s1_in[v].astype(F32)

    def c3(peer, src):
        return rdma(s3.at[src], s3.at[src], S3, peer, src, at_zo(peer))

    s3[zo] = part[...].astype(BF)
    pl.semaphore_wait(far, 1)
    for d in (2, 1, 3):
        c3((zo + d) % 4, zo).start()
    for d in (1, 3, 2):
        c3(zo, (zo + d) % 4).wait_recv()
    g1[own] = (s3[0].astype(F32) + s3[1].astype(F32) + s3[2].astype(F32) + s3[3].astype(F32)).astype(BF)

    def c5(peer, src):
        return rdma(g1.at[src], g1.at[src], G1, peer, src, at_shard(peer))

    for d in hops:
        c5((own + d) % 8, own).start()
    for d in hops[::-1]:
        c5(own, (own + d) % 8).wait_recv()
    for q in range(8):
        skip = 0 if q % 2 == 0 else 2 * n2 - n1
        lo = (q // 4) * n1 + (q % 2) * n2
        fin[at(mine + lo, n2 - skip), (q // 2 % 2) * half:(q // 2 % 2 + 1) * half] = g1[q, skip:, :]

    def c6(base, side, dev):
        blk = fin.at[at(base + side * n_quarter, n_quarter)]
        return rdma(blk, blk, G0, side, side, dev)

    c6(mine, 0, up).start()
    c6(mine, 1, down).start()
    c6(other, 0, up).wait_recv()
    c6(other, 1, down).wait_recv()
    stores[2].start()

    @pl.when(x >= 2)
    def _():
        @pl.when(x == 2)
        def _():
            for piece in (0, 1):
                ag(x, x + 1, piece).wait_send()

    @pl.when(x < 2)
    def _():
        for piece in (0, 1):
            ag(x, x + 2, piece).wait_send()

    @pl.when(k == 0)
    def _():
        own_fwd.wait_send()

    @pl.when(k == 1)
    def _():
        to_sib(x).wait_send()

    def drain(v, carry):
        pass_on(v, k).wait_send()
        lift(v, mine).wait_send()
        lower(v, mine).wait_send()
        to_sib(v).wait_send()
        to_up(v).wait_send()
        to_down(v).wait_send()
        to_x(v, x).wait_send()
        return carry

    lax.fori_loop(0, x, drain, 0)
    to_up(x).wait_send()
    to_down(x).wait_send()
    for d in hops:
        c1((own + d) % 8, own).wait_send()
        c5((own + d) % 8, own).wait_send()
    for d in (1, 2, 3):
        c3((zo + d) % 4, zo).wait_send()
    c6(mine, 0, up).wait_send()
    c6(mine, 1, down).wait_send()
    for store in stores:
        store.wait()


def write_out(a, b, c, a_out, b_out, c_out, a_v, b_v, c_v, wide, sems):
    loads = [
        pltpu.make_async_copy(src, dst, sems.at[i])
        for i, (src, dst) in enumerate(((c, c_v), (b, b_v), (a, a_v)))
    ]
    stores = [
        pltpu.make_async_copy(src, dst, sems.at[3 + i])
        for i, (src, dst) in enumerate(((wide, c_out), (b_v, b_out), (a_v, a_out)))
    ]
    for load in loads:
        load.start()
    loads[0].wait()
    wide[...] = c_v[...].astype(F32)
    stores[0].start()
    for i in (1, 2):
        loads[i].wait()
        stores[i].start()
    for store in stores:
        store.wait()


def body(queries, latents, out_grad):
    rows, _, feat = queries.shape
    lat = out_grad.shape[2]
    n1 = feat // 4
    n2 = (n1 // 2 + 15) // 16 * 16
    half = rows // 2
    qt = queries.reshape(rows, feat).T
    vm = pltpu.VMEM
    shapes = (
        jax.ShapeDtypeStruct((rows, lat), BF),
        jax.ShapeDtypeStruct((feat, rows), F32),
    )
    results = pl.pallas_call(
        kernel,
        out_shape=shapes + (jax.ShapeDtypeStruct((feat, rows), BF),),
        in_specs=[pl.BlockSpec(memory_space=pl.ANY)] * 3,
        out_specs=[pl.BlockSpec(memory_space=pl.ANY)] * 3,
        scratch_shapes=[
            vm((rows, lat), BF),
            vm((feat, rows), F32),
            vm((feat, rows), BF),
            vm((feat, rows), BF),
            vm((feat, rows), BF),
            vm((rows, lat), BF),
            vm((8, feat, rows), BF),
            vm((rows, feat), BF),
            vm((lat, rows), BF),
            vm((8, rows, rows), F32),
            vm((8, rows, rows), F32),
            vm((rows, lat), F32),
            vm((rows, 1), F32),
            vm((rows, 1), F32),
            vm((4, feat, rows), BF),
            vm((4, feat, rows), BF),
            vm((4, feat, rows), F32),
            vm((4, feat // 2, rows), BF),
            vm((4, feat // 2, rows), BF),
            vm((4, feat // 2, rows), BF),
            vm((4, feat // 2, rows), BF),
            vm((feat // 2, rows), F32),
            vm((8, n2, half), BF),
            vm((8, n2, half), BF),
            vm((n2, half), F32),
            vm((4, n2, half), BF),
            vm((8, n2, half), BF),
            pltpu.SemaphoreType.DMA((3,)),
            pltpu.SemaphoreType.DMA((3,)),
            pltpu.SemaphoreType.DMA((26, 8)),
            pltpu.SemaphoreType.REGULAR,
        ],
        compiler_params=pltpu.CompilerParams(
            collective_id=0, has_side_effects=True, vmem_limit_bytes=60 * 2**20
        ),
    )(qt, latents.T, out_grad.reshape(rows, lat))
    att, qg, lg = pl.pallas_call(
        write_out,
        out_shape=shapes + (jax.ShapeDtypeStruct((feat, rows), F32),),
        in_specs=[pl.BlockSpec(memory_space=pl.ANY)] * 3,
        out_specs=[pl.BlockSpec(memory_space=pl.ANY)] * 3,
        scratch_shapes=[
            vm((rows, lat), BF),
            vm((feat, rows), F32),
            vm((feat, rows), BF),
            vm((feat, rows), F32),
            pltpu.SemaphoreType.DMA((6,)),
        ],
        compiler_params=pltpu.CompilerParams(vmem_limit_bytes=60 * 2**20),
    )(*results)
    return att.reshape(rows, 1, lat), qg.T.reshape(rows, 1, feat), lg.T


def solution(mesh):
    return jax.shard_map(
        body,
        mesh=mesh,
        in_specs=(
            P(("rep", "exp"), "ctx", None),
            P(("rep", "exp"), None),
            P(("rep", "exp"), "ctx", None),
        ),
        out_specs=(
            P(("rep", "exp"), "ctx", None),
            P(("rep", "exp"), "ctx", None),
            P(("rep", "exp"), None),
        ),
        check_vma=False,
    )
```

time: 95.6 us -> 84.4 us (0.88)
  the two profiles are of different devices: /device:TPU:52 before, /device:TPU:16 now
where the time goes in v2:
time: 84.4 us; the launch traced here: 84.2 us
  Pallas kernels  83.6 us (99%)
    pallas_call x1, Pallas kernels, body(): pl.pallas_call(kernel, out_shape=shapes + (jax.ShapeDtypeStruct((feat, ro...  81.4 us
    pallas_call x1, Pallas kernels, body(): pl.pallas_call(write_out, out_shape=shapes + (jax.ShapeDtypeStruct((feat,...  2.14 us

profile of v2, /device:TPU:16, one launch (start us, length us, event | category | flops | bytes accessed | tf_op | source)
XLA Modules:
  0.0 84.2 jit_solution(12801477178704079280)
XLA Ops:
  0.6 81.4 %shard_map.58 = (bf16[256,512]{1,0:T(8,128)(2,1)}, f32[576,256]{1,0:T(8,128)}, bf16[576,256]{1,0:T(8,128)(2,1)}) custom-call(bf16[576,256]{1,0:T(8,128)(2,1)} %bitcast.10, bf16[576,256]{1,0:T(8,128)(2,1)} %bitcast.11, bf16[256,512]{1,0:T(8,128)(2,1)} %bitcast.12), custom_call_target="tpu_custom_call" | custom-call | tf_op jit(solution)/shard_map/pallas_call | solution.py:416
  82.1 2.1 %shard_map.59 = (bf16[256,512]{1,0:T(8,128)(2,1)}, f32[576,256]{1,0:T(8,128)}, f32[576,256]{1,0:T(8,128)}) custom-call(bf16[256,512]{1,0:T(8,128)(2,1)} %get-tuple-element.9.a, f32[576,256]{1,0:T(8,128)} %get-tuple-element.10.b, bf16[576,256]{1,0:T(8,128)(2,1)} %get-tuple-element.11.c), custom_call_target="tpu_custom_call" | custom-call | tf_op jit(solution)/shard_map/pallas_call | solution.py:458

commit v3 on v2

--- a/solution.py
+++ b/solution.py
@@ -32,7 +32,7 @@
     keys, qn, gt, sc, pg, ctx, row_m, row_l,
     sib_out, sib_in, hold, z_out, z_in, x_out, x_in, total,
     s1_out, s1_in, part, s3, g1,
-    in_sem, out_sem, sem, far,
+    in_sem, out_sem, sem, told,
 ):
     c = lax.axis_index("ctx")
     e = lax.axis_index("exp")
@@ -76,14 +76,22 @@
         )
 
     barrier = pltpu.get_barrier_semaphore()
-    near = [sib, up, down, at_zo((zo + 1) % 4), at_zo((zo + 3) % 4)]
-    near += [at_x((x + d) % 4) for d in (1, 2, 3)] + [at_shard((own + d) % 8) for d in range(1, 8)]
-    for dev in near:
-        pl.semaphore_signal(barrier, inc=1, device_id=dev, device_id_type=MESH)
+    def at_z(v):
+        return {"ctx": yh * 16 + v % 16}
+
+    def at_y(v):
+        return {"ctx": (v % 4) * 16 + z}
+
+    def tell(sem_ref, devices):
+        for dev in devices:
+            pl.semaphore_signal(sem_ref, inc=1, device_id=dev, device_id_type=MESH)
+
+    near = [at_x((x + d) % 4) for d in (1, 2, 3)] + [sib, up, down, at_y(yh + 1), at_y(yh + 3)]
+    tell(barrier, near)
     loads[0].wait()
     keys[e] = lt_ref[...]
     pl.semaphore_wait(barrier, len(near))
-    pl.semaphore_signal(far, inc=1, device_id=at_zo((zo + 1) % 4), device_id_type=MESH)
+    tell(told.at[0], [up, down, at_y(yh + 1)])
 
     def ag(src_x, dst_x, piece):
         part = at(mine + piece * n_quarter, n_quarter)
@@ -161,23 +169,36 @@
         own_fwd.wait_recv()
         forward(x * 2)
 
-    def gather_step(i, carry):
-        v = x - jnp.where(i == 0, 1, jnp.where(i == 1, 3, 2))
-
-        @pl.when((i < 3) & (v >= 0))
+    def source(i):
+        return x - jnp.where(i == 0, 1, jnp.where(i == 1, 3, 2))
+
+    def share_step(i, carry):
+        v = source(i)
+
+        @pl.when(v >= 0)
         def _():
             ag(v, x, 0).wait_recv()
             lift(v, mine).start()
             ag(v, x, 1).wait_recv()
             lower(v, mine).start()
 
-        w = x - jnp.where(i == 1, 1, jnp.where(i == 2, 3, 2))
+        return carry
+
+    lax.fori_loop(0, 3, share_step, 0)
+
+    def gather_step(i, carry):
+        v = source(i)
+
+        @pl.when((i < 3) & (v >= 0))
+        def _():
+            lift(v, other).wait_recv()
+            lower(v, other).wait_recv()
+            pass_on(v, k).start()
+
+        w = source(i - 1)
 
         @pl.when((i > 0) & (w >= 0))
         def _():
-            lift(w, other).wait_recv()
-            lower(w, other).wait_recv()
-            pass_on(w, k).start()
             forward(w * 2 + k)
             pass_on(w, 1 - k).wait_recv()
             forward(w * 2 + 1 - k)
@@ -185,6 +206,8 @@
         return carry
 
     lax.fori_loop(0, 4, gather_step, 0)
+    pl.semaphore_wait(told.at[0], 3)
+    tell(told.at[1], [at_y(yh + 1), at_y(yh + 2), at_y(yh + 3), at_z(z + 2), at_z(z + 14)])
 
     inv = 1.0 / row_l[...]
     context = ctx[...] * inv
@@ -218,10 +241,20 @@
     def order(i):
         return x - jnp.where(i == 0, 2, jnp.where(i == 1, 3, jnp.where(i == 2, 1, 0)))
 
+    def share_sum(u):
+        @pl.when(u * 2 + k <= x * 2 + 1 - k)
+        def _():
+            to_sib(u).wait_recv()
+            hold[u] += sib_in[u].astype(F32)
+
+        z_out[u] = hold[u, at(other, n_half), :].astype(BF)
+        to_up(u).start()
+        to_down(u).start()
+
     def bwd_step(i, carry):
         v = order(i)
 
-        @pl.when((i < 4) & (v >= 0))
+        @pl.when(v >= 0)
         def _():
             def put_sib(lo, hi, val):
                 sib_out[v, lo:hi, :] = val.astype(BF)
@@ -238,20 +271,22 @@
 
         u = order(i - 1)
 
-        @pl.when((i > 0) & (i < 5) & (u >= 0))
-        def _():
-            @pl.when(u * 2 + k <= x * 2 + 1 - k)
-            def _():
-                to_sib(u).wait_recv()
-                hold[u] += sib_in[u].astype(F32)
-
-            z_out[u] = hold[u, at(other, n_half), :].astype(BF)
-            to_up(u).start()
-            to_down(u).start()
-
-        t = order(i - 2)
-
-        @pl.when((i > 1) & (t >= 0))
+        @pl.when((i > 0) & (u >= 0))
+        def _():
+            share_sum(u)
+
+        return carry
+
+    lax.fori_loop(0, 4, bwd_step, 0)
+
+    def send_step(i, carry):
+        t = order(i)
+
+        @pl.when(i == 2)
+        def _():
+            share_sum(x)
+
+        @pl.when(t >= 0)
         def _():
             to_down(t).wait_recv()
             to_up(t).wait_recv()
@@ -268,7 +303,9 @@
 
         return carry
 
-    lax.fori_loop(0, 6, bwd_step, 0)
+    lax.fori_loop(0, 4, send_step, 0)
+    pl.semaphore_wait(told.at[1], 5)
+    tell(told.at[2], [at_z(z + 4)])
     qg_ref[...] = qg_ref[...] * score_scale
     stores[1].start()
 
@@ -307,7 +344,7 @@
         return rdma(s3.at[src], s3.at[src], S3, peer, src, at_zo(peer))
 
     s3[zo] = part[...].astype(BF)
-    pl.semaphore_wait(far, 1)
+    pl.semaphore_wait(told.at[2], 1)
     for d in (2, 1, 3):
         c3((zo + d) % 4, zo).start()
     for d in (1, 3, 2):
@@ -449,7 +486,7 @@
             pltpu.SemaphoreType.DMA((3,)),
             pltpu.SemaphoreType.DMA((3,)),
             pltpu.SemaphoreType.DMA((26, 8)),
-            pltpu.SemaphoreType.REGULAR,
+            pltpu.SemaphoreType.REGULAR((3,)),
         ],
         compiler_params=pltpu.CompilerParams(
             collective_id=0, has_side_effects=True, vmem_limit_bytes=60 * 2**20

time: 84.4 us -> 78.9 us (0.935)
  the two profiles are of different devices: /device:TPU:16 before, /device:TPU:2 now
where the time goes in v3:
time: 78.9 us; the launch traced here: 78.7 us
  Pallas kernels  78.1 us (99%)
    pallas_call x1, Pallas kernels, body(): pl.pallas_call(kernel, out_shape=shapes + (jax.ShapeDtypeStruct((feat, ro...  75.9 us
    pallas_call x1, Pallas kernels, body(): pl.pallas_call(write_out, out_shape=shapes + (jax.ShapeDtypeStruct((feat,...  2.14 us

profile of v3, /device:TPU:2, one launch (start us, length us, event | category | flops | bytes accessed | tf_op | source)
XLA Modules:
  0.0 78.7 jit_solution(17564250635950618170)
XLA Ops:
  0.6 75.9 %shard_map.58 = (bf16[256,512]{1,0:T(8,128)(2,1)}, f32[576,256]{1,0:T(8,128)}, bf16[576,256]{1,0:T(8,128)(2,1)}) custom-call(bf16[576,256]{1,0:T(8,128)(2,1)} %bitcast.10, bf16[576,256]{1,0:T(8,128)(2,1)} %bitcast.11, bf16[256,512]{1,0:T(8,128)(2,1)} %bitcast.12), custom_call_target="tpu_custom_call" | custom-call | tf_op jit(solution)/shard_map/pallas_call | solution.py:453
  76.6 2.1 %shard_map.59 = (bf16[256,512]{1,0:T(8,128)(2,1)}, f32[576,256]{1,0:T(8,128)}, f32[576,256]{1,0:T(8,128)}) custom-call(bf16[256,512]{1,0:T(8,128)(2,1)} %get-tuple-element.9.a, f32[576,256]{1,0:T(8,128)} %get-tuple-element.10.b, bf16[576,256]{1,0:T(8,128)(2,1)} %get-tuple-element.11.c), custom_call_target="tpu_custom_call" | custom-call | tf_op jit(solution)/shard_map/pallas_call | solution.py:495

commit v4 on v3

--- a/solution.py
+++ b/solution.py
@@ -13,7 +13,7 @@
 score_scale = 192.0 ** (-0.5)
 NN = (((1,), (0,)), ((), ()))
 NT = (((1,), (1,)), ((), ()))
-(AG, AH, ZU, ZD, FS, CR, RU, RD, XR, S1, S3, G1, G0) = range(0, 26, 2)
+(AG, AH, ZU, ZD, FS, CR, RU, RD, XR, XQ, S1, S3, G1, G0) = range(0, 28, 2)
 
 
 def mm(a, b, dims=NN):
@@ -31,7 +31,7 @@
     qt_ref, lt_ref, g_ref,
     keys, qn, gt, sc, pg, ctx, row_m, row_l,
     sib_out, sib_in, hold, z_out, z_in, x_out, x_in, total,
-    s1_out, s1_in, part, s3, g1,
+    s1_out, s1_in, part, s3, g1, g0,
     in_sem, out_sem, sem, told,
 ):
     c = lax.axis_index("ctx")
@@ -235,8 +235,9 @@
     def to_down(v):
         return rdma(z_out.at[v, pl.ds(0, n_quarter)], z_in.at[v, pl.ds(0, n_quarter)], RD, v, v, down)
 
-    def to_x(v, src):
-        return rdma(x_out.at[v], x_in.at[src], XR, v, src, at_x(v))
+    def to_x(v, src, piece):
+        part = pl.ds(piece * n_quarter, n_quarter)
+        return rdma(x_out.at[v, part], x_in.at[src, part], XR if piece == 0 else XQ, v, src, at_x(v))
 
     def order(i):
         return x - jnp.where(i == 0, 2, jnp.where(i == 1, 3, jnp.where(i == 2, 1, 0)))
@@ -251,90 +252,100 @@
         to_up(u).start()
         to_down(u).start()
 
-    def bwd_step(i, carry):
+    def sib_step(i, carry):
         v = order(i)
 
-        @pl.when(v >= 0)
+        @pl.when((v >= 0) & (v * 2 + 1 - k <= e))
         def _():
             def put_sib(lo, hi, val):
                 sib_out[v, lo:hi, :] = val.astype(BF)
 
+            backward(v * 2 + 1 - k, put_sib)
+            to_sib(v).start()
+
+        return carry
+
+    lax.fori_loop(0, 4, sib_step, 0)
+
+    def own_step(i, carry):
+        v = order(i)
+
+        @pl.when(v >= 0)
+        def _():
             def put_hold(lo, hi, val):
                 hold[v, lo:hi, :] = val
 
-            @pl.when(v * 2 + 1 - k <= e)
+            backward(v * 2 + k, put_hold)
+
+            @pl.when(v < x)
             def _():
-                backward(v * 2 + 1 - k, put_sib)
-                to_sib(v).start()
-
-            backward(v * 2 + k, put_hold)
-
-        u = order(i - 1)
-
-        @pl.when((i > 0) & (u >= 0))
-        def _():
-            share_sum(u)
+                share_sum(v)
 
         return carry
 
-    lax.fori_loop(0, 4, bwd_step, 0)
-
-    def send_step(i, carry):
-        t = order(i)
-
-        @pl.when(i == 2)
-        def _():
-            share_sum(x)
-
-        @pl.when(t >= 0)
-        def _():
-            to_down(t).wait_recv()
-            to_up(t).wait_recv()
-            val = hold[t, at(mine, n_half), :] + z_in[t].astype(F32)
-
-            @pl.when(t < x)
+    lax.fori_loop(0, 4, own_step, 0)
+
+    def pair_sum(t, piece):
+        lo = piece * n_quarter
+        return hold[t, at(mine + lo, n_quarter), :] + z_in[t, lo:lo + n_quarter, :].astype(F32)
+
+    def send_step(piece):
+        def step(i, carry):
+            t = order(i)
+
+            @pl.when(t >= 0)
             def _():
-                x_out[t] = val.astype(BF)
-                to_x(t, x).start()
-
-            @pl.when(t == x)
-            def _():
-                total[...] = val
-
-        return carry
-
-    lax.fori_loop(0, 4, send_step, 0)
+                (to_down, to_up)[piece](t).wait_recv()
+                x_out[t, piece * n_quarter:(piece + 1) * n_quarter, :] = pair_sum(t, piece).astype(BF)
+                to_x(t, x, piece).start()
+
+            return carry
+
+        lax.fori_loop(0, 3, step, 0)
+
+    send_step(0)
+    share_sum(x)
+    send_step(1)
     pl.semaphore_wait(told.at[1], 5)
     tell(told.at[2], [at_z(z + 4)])
     qg_ref[...] = qg_ref[...] * score_scale
     stores[1].start()
 
-    def add_x(i, carry):
-        v = 3 - i
-        to_x(x, v).wait_recv()
-        total[...] += x_in[v].astype(F32)
-        return carry
-
-    lax.fori_loop(0, 3 - x, add_x, 0)
+    to_down(x).wait_recv()
+    total[:n_quarter, :] = pair_sum(x, 0)
+    to_up(x).wait_recv()
+    total[n_quarter:, :] = pair_sum(x, 1)
 
     half = rows // 2
-    n1, n2 = n_half // 2, s1_out.shape[1]
+    n1, n2 = n_quarter, s1_out.shape[1]
 
     def c1(peer, src):
         return rdma(s1_out.at[peer], s1_in.at[src], S1, peer, src, at_shard(peer))
 
-    for q in range(8):
-        lo = (q // 4) * n1 + (q % 2) * (n1 - n2)
-        val = total[lo:lo + n2, (q // 2 % 2) * half:(q // 2 % 2 + 1) * half]
-        s1_out[q] = val.astype(BF)
-
-        @pl.when(own == q)
-        def _():
-            part[...] = val
+    for piece in (0, 1):
+        span = slice(piece * n_quarter, (piece + 1) * n_quarter)
+
+        def add_x(i, carry):
+            v = 3 - i
+            to_x(x, v, piece).wait_recv()
+            total[span, :] += x_in[v, span, :].astype(F32)
+            return carry
+
+        lax.fori_loop(0, 3 - x, add_x, 0)
+        for q in range(piece * 4, piece * 4 + 4):
+            lo = piece * n1 + (q % 2) * (n1 - n2)
+            val = total[lo:lo + n2, (q // 2 % 2) * half:(q // 2 % 2 + 1) * half]
+
+            @pl.when(own == q)
+            def _():
+                part[...] = val
+
+            @pl.when(own != q)
+            def _():
+                s1_out[q] = val.astype(BF)
+                c1(q, own).start()
 
     hops = (4, 5, 3, 2, 6, 7, 1)
-    for d in hops:
-        c1((own + d) % 8, own).start()
     for d in hops[::-1]:
         v = (own + d) % 8
         c1(own, v).wait_recv()
@@ -345,34 +356,15 @@
 
     s3[zo] = part[...].astype(BF)
     pl.semaphore_wait(told.at[2], 1)
-    for d in (2, 1, 3):
-        c3((zo + d) % 4, zo).start()
-    for d in (1, 3, 2):
-        c3(zo, (zo + d) % 4).wait_recv()
-    g1[own] = (s3[0].astype(F32) + s3[1].astype(F32) + s3[2].astype(F32) + s3[3].astype(F32)).astype(BF)
-
-    def c5(peer, src):
-        return rdma(g1.at[src], g1.at[src], G1, peer, src, at_shard(peer))
-
-    for d in hops:
-        c5((own + d) % 8, own).start()
-    for d in hops[::-1]:
-        c5(own, (own + d) % 8).wait_recv()
-    for q in range(8):
-        skip = 0 if q % 2 == 0 else 2 * n2 - n1
-        lo = (q // 4) * n1 + (q % 2) * n2
-        fin[at(mine + lo, n2 - skip), (q // 2 % 2) * half:(q // 2 % 2 + 1) * half] = g1[q, skip:, :]
-
-    def c6(base, side, dev):
-        blk = fin.at[at(base + side * n_quarter, n_quarter)]
-        return rdma(blk, blk, G0, side, side, dev)
-
-    c6(mine, 0, up).start()
-    c6(mine, 1, down).start()
-    c6(other, 0, up).wait_recv()
-    c6(other, 1, down).wait_recv()
-    stores[2].start()
-
+    @pl.when(zo != 0)
+    def _():
+        c3(0, zo).start()
+        c3(0, zo).wait_send()
+
+    for q in (1, 2, 3):
+        @pl.when(zo != q)
+        def _():
+            c3(q, zo).start()
     @pl.when(x >= 2)
     def _():
         @pl.when(x == 2)
@@ -400,7 +392,8 @@
         to_sib(v).wait_send()
         to_up(v).wait_send()
         to_down(v).wait_send()
-        to_x(v, x).wait_send()
+        to_x(v, x, 0).wait_send()
+        to_x(v, x, 1).wait_send()
         return carry
 
     lax.fori_loop(0, x, drain, 0)
@@ -408,13 +401,57 @@
     to_down(x).wait_send()
     for d in hops:
         c1((own + d) % 8, own).wait_send()
+    stores[0].wait()
+    stores[1].wait()
+    for d in (1, 3, 2):
+        c3(zo, (zo + d) % 4).wait_recv()
+    g1[own] = (s3[0].astype(F32) + s3[1].astype(F32) + s3[2].astype(F32) + s3[3].astype(F32)).astype(BF)
+
+    def c5(peer, src):
+        return rdma(g1.at[src], g1.at[src], G1, peer, src, at_shard(peer))
+
+    def c6(q, dev):
+        return rdma(g1.at[q], g0.at[q], G0, q, q, dev)
+
+    def relay(q):
+        @pl.when(q < 4)
+        def _():
+            c6(q, up).start()
+
+        @pl.when(q >= 4)
+        def _():
+            c6(q, down).start()
+
+    for d in hops:
+        c5((own + d) % 8, own).start()
+    relay(own)
+    for d in hops[::-1]:
+        v = (own + d) % 8
+        c5(own, v).wait_recv()
+        relay(v)
+
+    def place(base, shards, q):
+        skip = 0 if q % 2 == 0 else 2 * n2 - n1
+        lo = (q // 4) * n1 + (q % 2) * n2
+        fin[at(base + lo, n2 - skip), (q // 2 % 2) * half:(q // 2 % 2 + 1) * half] = shards[q, skip:, :]
+
+    for q in range(8):
+        place(mine, g1, q)
+    for q in range(8):
+        c6(q, up if q < 4 else down).wait_recv()
+        place(other, g0, q)
+    stores[2].start()
+
+    for d in hops:
         c5((own + d) % 8, own).wait_send()
-    for d in (1, 2, 3):
-        c3((zo + d) % 4, zo).wait_send()
-    c6(mine, 0, up).wait_send()
-    c6(mine, 1, down).wait_send()
-    for store in stores:
-        store.wait()
+    for q in (1, 2, 3):
+        @pl.when(zo != q)
+        def _():
+            c3(q, zo).wait_send()
+
+    for q in range(8):
+        c6(q, up if q < 4 else down).wait_send()
+    stores[2].wait()
 
 
 def write_out(a, b, c, a_out, b_out, c_out, a_v, b_v, c_v, wide, sems):
@@ -483,9 +520,10 @@
             vm((n2, half), F32),
             vm((4, n2, half), BF),
             vm((8, n2, half), BF),
+            vm((8, n2, half), BF),
             pltpu.SemaphoreType.DMA((3,)),
             pltpu.SemaphoreType.DMA((3,)),
-            pltpu.SemaphoreType.DMA((26, 8)),
+            pltpu.SemaphoreType.DMA((28, 8)),
             pltpu.SemaphoreType.REGULAR((3,)),
         ],
         compiler_params=pltpu.CompilerParams(

time: 78.9 us -> 78.7 us (level)
  the two profiles are of different devices: /device:TPU:2 before, /device:TPU:18 now
where the time goes in v4:
time: 78.7 us; the launch traced here: 78.6 us
  Pallas kernels  77.9 us (99%)
    pallas_call x1, Pallas kernels, body(): pl.pallas_call(kernel, out_shape=shapes + (jax.ShapeDtypeStruct((feat, ro...  75.8 us
    pallas_call x1, Pallas kernels, body(): pl.pallas_call(write_out, out_shape=shapes + (jax.ShapeDtypeStruct((feat,...  2.14 us

profile of v4, /device:TPU:18, one launch (start us, length us, event | category | flops | bytes accessed | tf_op | source)
XLA Modules:
  0.0 78.6 jit_solution(8794804659786668839)
XLA Ops:
  0.6 75.8 %shard_map.58 = (bf16[256,512]{1,0:T(8,128)(2,1)}, f32[576,256]{1,0:T(8,128)}, bf16[576,256]{1,0:T(8,128)(2,1)}) custom-call(bf16[576,256]{1,0:T(8,128)(2,1)} %bitcast.10, bf16[576,256]{1,0:T(8,128)(2,1)} %bitcast.11, bf16[256,512]{1,0:T(8,128)(2,1)} %bitcast.12), custom_call_target="tpu_custom_call" | custom-call | tf_op jit(solution)/shard_map/pallas_call | solution.py:490
  76.4 2.1 %shard_map.59 = (bf16[256,512]{1,0:T(8,128)(2,1)}, f32[576,256]{1,0:T(8,128)}, f32[576,256]{1,0:T(8,128)}) custom-call(bf16[256,512]{1,0:T(8,128)(2,1)} %get-tuple-element.9.a, f32[576,256]{1,0:T(8,128)} %get-tuple-element.10.b, bf16[576,256]{1,0:T(8,128)(2,1)} %get-tuple-element.11.c), custom_call_target="tpu_custom_call" | custom-call | tf_op jit(solution)/shard_map/pallas_call | solution.py:533
